TPU v7x, 32 devices: a whole 2x2x4 slice. The times are simulated.
32 devices in a mesh: gz: 4 (over y, core), xy: 8 (over z, x).
Axes of the slice: x: 2, y: 2, z: 4, core: 2. Of those that a mesh axis runs over, the one named last changes fastest.
Arguments:
- cotangent: bfloat16 [4, 8, 9, 128, 128], P('gz', 'xy'), may hold values from -6 to 6
- displacement: float32 [4, 8, 3, 32, 128], P('gz', 'xy'), may hold values from -2 to 2
- neighbours: int32 [4, 8, 32, 128], P('gz', 'xy'), may hold values from 0 to 2303
- counts: int32 [4, 8, 128], P('gz', 'xy'), may hold values from 8 to 32, as said below
- atom_feat: bfloat16 [4, 8, 256, 128], P('gz', 'xy'), may hold values from -6 to 6
- radial_weight: float32 [3, 16, 128], replicated, may hold values from -1.5 to 1.5
- mix_weight: bfloat16 [3, 128, 128], replicated, may hold values from -0.5 to 0.5
Outputs:
- atom_grad: float32 [4, 8, 256, 128], P('gz', 'xy')
- radial_grad: float32 [3, 16, 128], replicated
- mix_grad: float32 [3, 128, 128], replicated
Inputs may be any that keep to these rules, and one draw needn't show every extreme that they name: `counts`: the first probe of the first brick uses all 32 slots and the first probe of the second brick uses 32 // 4.
All inputs are finite; a program needn't handle non-finite values.
Results may differ from a plain program's by a relative error of at most 0.0051.
Values may be sent and summed in bfloat16 or wider, within the bound.
A program may use at most 64 MiB of HBM per device.

v0:
```python
import math

import jax
import jax.numpy as jnp
from jax import lax
from jax.sharding import PartitionSpec as P

CUTOFF = 4.0
LEVEL_SPANS = ((0, 1), (1, 4), (4, 9))


def padded(cells, sides, width):
    for axis, dim in sides:
        count = lax.axis_size(axis)
        head = lax.slice_in_dim(cells, 0, width, axis=dim)
        tail = lax.slice_in_dim(cells, cells.shape[dim] - width, cells.shape[dim], axis=dim)
        cells = jnp.concatenate(
            [
                lax.ppermute(tail, axis, [(i, (i + 1) % count) for i in range(count)]),
                cells,
                lax.ppermute(head, axis, [((i + 1) % count, i) for i in range(count)]),
            ],
            axis=dim,
        )
    return cells


def harmonics(disp):
    scaled = disp / CUTOFF
    coord_x, coord_y, coord_z = (scaled[0], scaled[1], scaled[2])
    root3, root5, root15 = (math.sqrt(3.0), math.sqrt(5.0), math.sqrt(15.0))
    return jnp.stack(
        [
            jnp.ones_like(coord_x),
            root3 * coord_x,
            root3 * coord_y,
            root3 * coord_z,
            root15 * coord_x * coord_y,
            root15 * coord_y * coord_z,
            0.5 * root5 * (2.0 * coord_z * coord_z - coord_x * coord_x - coord_y * coord_y),
            root15 * coord_x * coord_z,
            0.5 * root15 * (coord_x * coord_x - coord_y * coord_y),
        ]
    )


def basis(disp, nbasis):
    distance = jnp.sqrt(jnp.sum(disp * disp, axis=0))
    centres = jnp.arange(nbasis).astype(jnp.float32) * (CUTOFF / (nbasis - 1))
    sharpness = ((nbasis - 1) / CUTOFF) ** 2
    envelope = 0.5 * (jnp.cos(math.pi * distance / CUTOFF) + 1.0)
    shaped = centres.reshape((nbasis,) + (1,) * distance.ndim)
    return jnp.exp(-sharpness * (distance[None] - shaped) ** 2) * envelope[None]


def exact(form, left, right):
    return jnp.einsum(form, left, right, precision=lax.Precision.HIGHEST)


def matmul(form, left, right):
    return jnp.einsum(form, left, right, preferred_element_type=jnp.float32)


def gate_backward(moments, mix_weight, cotangent):
    mixed_out = [
        matmul("mpc,cd->mpd", moments[span_start:span_end], mix_weight[level])
        for level, (span_start, span_end) in enumerate(LEVEL_SPANS)
    ]
    scalar = mixed_out[0][0]
    gating = jax.nn.sigmoid(scalar)
    gate_slope = gating * (1.0 - gating)
    cot_float = cotangent.astype(jnp.float32)
    higher = jnp.concatenate(mixed_out[1:], 0)
    first_term = (
        cot_float[0] * (gating + scalar * gate_slope)
        + jnp.sum(cot_float[1:] * higher, 0) * gate_slope
    )
    dmixed = jnp.concatenate([first_term[None], cot_float[1:] * gating[None]], 0).astype(
        jnp.bfloat16
    )
    dmoments = jnp.concatenate(
        [
            matmul("mpd,cd->mpc", dmixed[span_start:span_end], mix_weight[level])
            for level, (span_start, span_end) in enumerate(LEVEL_SPANS)
        ],
        0,
    ).astype(jnp.bfloat16)
    mix_part = jnp.stack(
        [
            matmul("mpc,mpd->cd", moments[span_start:span_end], dmixed[span_start:span_end])
            for span_start, span_end in LEVEL_SPANS
        ]
    )
    return (dmoments, mix_part)


def shards(cotangent, displacement, neighbours, counts, atom_feat, radial_weight, mix_weight):
    cot_local = cotangent[0, 0]
    disp_local = displacement[0, 0]
    neighbour_local_index = neighbours[0, 0]
    probe_tally = counts[0, 0]
    slot_count = neighbour_local_index.shape[0]
    probe_count = neighbour_local_index.shape[1]
    natom = atom_feat.shape[2]
    channels = atom_feat.shape[3]
    nbasis = radial_weight.shape[1]
    filled_slots = (
        lax.broadcasted_iota(jnp.int32, (slot_count, probe_count), 0) < probe_tally[None]
    ).astype(jnp.float32)
    angular = harmonics(disp_local) * filled_slots[None]
    radial_basis = basis(disp_local, nbasis)
    atom_table = padded(atom_feat, (("gz", 0), ("xy", 1)), 1).reshape(9 * natom, channels)
    features = atom_table[neighbour_local_index].astype(jnp.float32)
    radial = exact("bkp,lbc->lkpc", radial_basis, radial_weight)
    pieces = []
    for level, (span_start, span_end) in enumerate(LEVEL_SPANS):
        weighted = radial[level] * features
        pieces.append(jnp.sum(angular[span_start:span_end, :, :, None] * weighted[None], axis=1))
    moments = jnp.concatenate(pieces, 0).astype(jnp.bfloat16)
    dmoments, mix_part = gate_backward(moments, mix_weight, cot_local)
    mix_total = lax.psum(mix_part, ("gz", "xy"))
    dmoment_float = dmoments.astype(jnp.float32)
    contrib = jnp.zeros(features.shape, jnp.float32)
    radial_parts = []
    for level, (span_start, span_end) in enumerate(LEVEL_SPANS):
        traced = jnp.sum(
            angular[span_start:span_end, :, :, None] * dmoment_float[span_start:span_end, None],
            axis=0,
        )
        contrib = contrib + radial[level] * traced
        radial_parts.append(exact("bkp,kpc->bc", radial_basis, features * traced))
    grads = (
        jnp.zeros((9 * natom, channels), jnp.float32)
        .at[neighbour_local_index.reshape(-1)]
        .add(contrib.reshape(-1, channels))
    )
    radial_part = jnp.stack(radial_parts)
    radial_total = lax.psum(radial_part, ("gz", "xy"))
    blocks = grads.reshape(3, 3, natom, channels)
    outer_rows = jnp.stack([blocks[0], blocks[2]], 0)
    arrived = padded(outer_rows, (("gz", 0),), 1)
    columns = blocks[1] + arrived[0] + arrived[3]
    outer_columns = jnp.stack([columns[0], columns[2]], 0)
    landed = padded(outer_columns, (("xy", 0),), 1)
    owned = columns[1] + landed[0] + landed[3]
    return (owned[None, None], radial_total, mix_total)


def solution(mesh):
    in_specs = (
        P("gz", "xy", None, None, None),
        P("gz", "xy", None, None, None),
        P("gz", "xy", None, None),
        P("gz", "xy", None),
        P("gz", "xy", None, None),
        P(),
        P(),
    )
    out_specs = (P("gz", "xy", None, None), P(), P())
    return jax.shard_map(shards, mesh=mesh, in_specs=in_specs, out_specs=out_specs, check_vma=False)
```

profile of v0, /device:TPU:0, one launch (start us, length us, event | category | flops | bytes accessed | tf_op | source)
XLA Modules:
  0.0 236.9 jit_solution(9430039311791269466)
XLA Ops:
  7.2 0.0 copy-start
  7.2 0.0 all-reduce.2.cloned.1.call-start
  7.2 0.5 collective-permute-start
  7.7 2.0 collective-permute-start.1
  9.8 0.8 multiply_reduce_fusion.5
  10.7 0.7 fusion.78
  11.3 0.1 fusion.86
  11.4 1.3 compare_select_fusion
  12.8 0.0 copy-done
  12.8 0.0 copy-start.4
  12.8 0.0 copy-start.6
  12.8 0.0 copy-start.7
  12.8 7.2 %convolution_bitcast_fusion = f32[3,32,128,128]{3,2,0,1:T(8,128)} fusion(f32[32,128]{1,0:T(8,128)S(1)} %get-tuple-element.23, f32[16]{0:T(128)S(1)} %convert_multiply_fusion, f32[32,128]{1,0:T(8,128)S(1)} %get-tuple-element.22, f32[3,16,128]{2,1,0:T(8,128)S(1)} %copy-done), kind=kOutput, calls=%fused_computation.6 | convolution fusion | flops 302252032 | bytes 6348864 | tf_op jit(solution)/shard_map/bkp,lbc->lkpc/dot_general | solution.py:57
  20.1 0.0 copy-done.4
  20.1 0.9 convert_element_type.43
  21.0 0.0 collective-permute-done
  21.0 0.0 collective-permute-done.1
  21.0 2.3 collective-permute-start.2
  23.3 3.3 %collective-permute-start.3 = (bf16[3,1,256,128]{3,2,1,0:T(8,128)(2,1)S(1)}, bf16[3,1,256,128]{3,2,1,0:T(8,128)(2,1)S(1)}, u32[]{:S(2)}, u32[]{:S(2)}) collective-permute-start(bf16[3,1,256,128]{3,2,1,0:T(8,128)(2,1)S(1)} %constant_dynamic-update-slice_fusion.9), channel_id=1, source_target_pairs={{1,0},{2,1},{3,2},{4,3},{5,4},{6,5},{7,6},{0,7},{9,8},{10,9},{11,1... | collective-permute-start | bytes 589832 | tf_op jit(solution)/shard_map/ppermute | solution.py:21
  26.6 5.1 %collective-permute-done.2 = bf16[3,1,256,128]{3,2,1,0:T(8,128)(2,1)S(1)} collective-permute-done((bf16[3,1,256,128]{3,2,1,0:T(8,128)(2,1)S(1)}, bf16[3,1,256,128]{3,2,1,0:T(8,128)(2,1)S(1)}, u32[]{:S(2)}, u32[]{:S(2)}) %collective-permute-start.2) | collective-permute-done | bytes 196640 | tf_op jit(solution)/shard_map/ppermute | solution.py:19
  31.7 2.2 collective-permute-done.3
  34.0 0.1 pad_maximum_fusion
  34.0 12.1 %gather_fusion = bf16[4096,128]{1,0:T(8,128)(2,1)S(1)} fusion(bf16[2304,128]{1,0:T(8,128)(2,1)S(1)} %bitcast.167, s32[4096]{0:T(1024)S(1)} %fusion.74), kind=kCustom, calls=%fused_computation | custom fusion | bytes 2113536 | tf_op jit(solution)/shard_map/gather | solution.py:113
  46.2 0.1 convert_element_type.49
  46.3 3.6 %fusion.83 = (f32[1,32,128,128]{3,2,0,1:T(8,128)S(1)}, bf16[128,128]{1,0:T(8,128)(2,1)S(1)}, f32[32,128,128]{2,1,0:T(8,128)S(1)}, f32[32,128,128]{2,1,0:T(8,128)...) fusion(f32[3,32,128,128]{3,2,0,1:T(8,128)} %convolution_bitcast_fusion, ...), kind=kLoop, calls=%fused_computation.141 | loop fusion | flops 3129344 | bytes 19972096 | tf_op jit(solution)/shard_map/slice | solution.py:130
  49.9 0.0 copy-start.5
  49.9 2.0 multiply_reduce_fusion.3
  51.9 0.2 fusion.54
  52.1 3.1 %multiply_reduce_fusion.1 = bf16[5,128,128]{2,1,0:T(8,128)(2,1)S(1)} fusion(f32[32,128,128]{2,1,0:T(8,128)S(1)} %get-tuple-element.7, f32[5,32,128]{2,1,0:T(8,128)S(1)} %slice.162), kind=kLoop, calls=%fused_computation.3 | loop fusion | flops 5160960 | bytes 2342912 | tf_op jit(solution)/shard_map/reduce_sum | solution.py:118
  55.2 0.2 fusion.48
  55.4 0.2 add_divide_fusion
  55.6 0.1 fusion.24
  55.7 0.2 convolution_bitcast_fusion.2
  55.9 0.2 convolution_bitcast_fusion.1
  56.1 0.2 convolution_convert_fusion
  56.3 0.2 convolution_convert_fusion.1
  56.5 0.0 copy-start.9
  56.5 0.1 fusion.52
  56.6 0.1 fusion.10
  56.8 2.1 multiply_reduce_fusion.2
  58.9 2.1 fusion.11
  61.0 2.0 fusion.14
  63.0 3.2 %multiply_reduce_fusion = f32[32,128,128]{2,1,0:T(8,128)S(1)} fusion(f32[5,128,128]{2,1,0:T(8,128)S(1)} %fusion.27, f32[5,32,128]{2,1,0:T(8,128)S(1)} %slice.162), kind=kLoop, calls=%fused_computation.2 | loop fusion | flops 4718592 | bytes 2506752 | tf_op jit(solution)/shard_map/reduce_sum | solution.py:126
  66.3 2.4 %fusion = f32[4096,128]{1,0:T(8,128)} fusion(f32[32,128,128]{2,1,0:T(8,128)S(1)} %multiply_reduce_fusion, f32[1,32,128,128]{3,2,0,1:T(8,128)S(1)} %get-tuple-element.9, f32[32,128,128]{2,1,0:T(8,128)S(1)} %multiply_reduce_fusion.2, f32[1,32,128,128]{3,2,0,1:T(8,128)S(1)} %get-tuple-element.10, f32[1,32,128,128]{3,2,0,1:T(8,128)S(1)} %get-tuple-element.5, ...), kind=kLoop, calls=%fused_computation.8 | loop fusion | flops 3145728 | bytes 12664832 | tf_op jit(solution)/shard_map/add | solution.py:130
  68.7 22.9 %scatter_custom_fusion = f32[2304,128]{1,0:T(8,128)S(1)} fusion(s32[4096]{0:T(1024)} %bitcast.176, f32[4096,128]{1,0:T(8,128)} %fusion, f32[]{:T(128)} %constant.14.clone.1), kind=kCustom, calls=%fused_computation.36 | custom fusion | flops 524288 | bytes 1180160 | tf_op jit(solution)/shard_map/scatter-add | solution.py:135
  91.7 0.1 fusion.84
  91.8 0.1 collective-permute-start.4
  91.8 1.7 collective-permute-start.5
  93.6 0.2 convolution_bitcast_fusion.3
  93.8 1.3 fusion.17
  95.1 0.0 copy-start.10
  95.1 7.3 %collective-permute-done.4 = f32[1,3,256,128]{3,2,1,0:T(8,128)S(1)} collective-permute-done((f32[1,3,256,128]{3,2,1,0:T(8,128)S(1)}, f32[1,3,256,128]{3,2,1,0:T(8,128)S(1)}, u32[]{:S(2)}, u32[]{:S(2)}) %collective-permute-start.4) | collective-permute-done | bytes 393248 | tf_op jit(solution)/shard_map/ppermute | solution.py:19
  102.5 0.0 collective-permute-done.5
  102.5 0.1 bitcast_add_fusion
  102.6 0.3 collective-permute-start.6
  102.9 4.5 %collective-permute-start.7 = (f32[1,256,128]{2,1,0:T(8,128)S(1)}, f32[1,256,128]{2,1,0:T(8,128)S(1)}, u32[]{:S(2)}, u32[]{:S(2)}) collective-permute-start(f32[1,256,128]{2,1,0:T(8,128)S(1)} %get-tuple-element.17), channel_id=1, source_target_pairs={{1,0},{2,1},{3,2},{4,3},{5,4},{6,5},{7,6},{0,7},{9,8},{10,9},{11,1... | collective-permute-start | bytes 393224 | tf_op jit(solution)/shard_map/ppermute | solution.py:21
  107.3 0.7 pad_maximum_fusion.1
  108.0 0.0 all-reduce.2.cloned.1.call-update
  108.1 37.9 %psum.14 = f32[3,16,128]{2,1,0:T(8,128)} all-reduce(f32[3,16,128]{2,1,0:T(8,128)S(1)} %pad_maximum_fusion.4), channel_id=1, replica_groups=mesh['gz'=4,'xy'=8] {'gz','xy'}, use_global_device_ids=true, to_apply=%region_8.0 | all-reduce | flops 6144 | bytes 49152 | tf_op jit(solution)/shard_map/psum | solution.py:138
  146.0 0.0 collective-permute-done.6
  146.0 0.0 collective-permute-done.7
  146.0 0.7 fusion.29
  146.7 81.8 %all-reduce.2.cloned.1.call-done = f32[3,128,128]{2,1,0:T(8,128)} async-done(((f32[3,128,128]{2,1,0:T(8,128)}), f32[3,128,128]{2,1,0:T(8,128)}) %all-reduce.2.cloned.1.call-update) | async-done | bytes 196624 | tf_op jit(solution)/shard_map/psum | solution.py:121
  228.5 1.6 copy.28
  (40 shorter events, 0.3 us)
Async XLA Ops:
  7.2 5.6 %copy-start = (f32[3,16,128]{2,1,0:T(8,128)S(1)}, f32[3,16,128]{2,1,0:T(8,128)}, u32[]{:S(2)}) copy-start(f32[3,16,128]{2,1,0:T(8,128)} %param.12) | copy-start | bytes 73732
  7.2 221.3 %all-reduce.2.cloned.1.call-start = ((), (), s32[]{:S(2)}) async-start(), calls=%async_computation | async-start | bytes 393216 | tf_op jit(solution)/shard_map/psum | solution.py:121
  7.2 13.8 %collective-permute-start = (bf16[1,1,256,128]{3,2,1,0:T(8,128)(2,1)}, bf16[1,1,256,128]{3,2,1,0:T(8,128)(2,1)S(1)}, u32[]{:S(2)}, u32[]{:S(2)}) collective-permute-start(bf16[1,1,256,128]{3,2,1,0:T(8,128)(2,1)} %param.11), channel_id=1, source_target_pairs={{0,8},{8,16},{16,24},{24,0},{1,9},{9,17},{17,25},{25,1},{2,10},{10... | collective-permute-start | bytes 196616 | tf_op jit(solution)/shard_map/ppermute | solution.py:19
  7.7 13.3 %collective-permute-start.1 = (bf16[1,1,256,128]{3,2,1,0:T(8,128)(2,1)}, bf16[1,1,256,128]{3,2,1,0:T(8,128)(2,1)S(1)}, u32[]{:S(2)}, u32[]{:S(2)}) collective-permute-start(bf16[1,1,256,128]{3,2,1,0:T(8,128)(2,1)} %param.11), channel_id=1, source_target_pairs={{8,0},{16,8},{24,16},{0,24},{9,1},{17,9},{25,17},{1,25},{10,2},{18... | collective-permute-start | bytes 196616 | tf_op jit(solution)/shard_map/ppermute | solution.py:21
  9.8 49.2 %copy-start.11 = (f32[16]{0:T(128)}, f32[16]{0:T(128)S(1)}, u32[]{:S(2)}) copy-start(f32[16]{0:T(128)S(1)} %convert_multiply_fusion) | copy-start | bytes 196
  12.8 7.3 %copy-start.4 = (bf16[1,1,9,128,128]{4,3,2,1,0:T(8,128)(2,1)S(1)}, bf16[1,1,9,128,128]{4,3,2,1,0:T(8,128)(2,1)}, u32[]{:S(2)}) copy-start(bf16[1,1,9,128,128]{4,3,2,1,0:T(8,128)(2,1)} %param.7) | copy-start | bytes 884740
  12.8 8.2 %copy-start.6 = (bf16[1,1,256,128]{3,2,1,0:T(8,128)(2,1)S(1)}, bf16[1,1,256,128]{3,2,1,0:T(8,128)(2,1)}, u32[]{:S(2)}) copy-start(bf16[1,1,256,128]{3,2,1,0:T(8,128)(2,1)} %param.11) | copy-start | bytes 196612
  12.8 13.8 %copy-start.7 = (s32[1,1,32,128]{3,2,1,0:T(8,128)S(1)}, s32[1,1,32,128]{3,2,1,0:T(8,128)}, u32[]{:S(2)}) copy-start(s32[1,1,32,128]{3,2,1,0:T(8,128)} %param.9) | copy-start | bytes 49156
  20.1 26.3 %copy-start.8 = (f32[32,128]{1,0:T(8,128)}, f32[32,128]{1,0:T(8,128)S(1)}, u32[]{:S(2)}) copy-start(f32[32,128]{1,0:T(8,128)S(1)} %get-tuple-element.19) | copy-start | bytes 49156
  21.0 10.7 %collective-permute-start.2 = (bf16[3,1,256,128]{3,2,1,0:T(8,128)(2,1)S(1)}, bf16[3,1,256,128]{3,2,1,0:T(8,128)(2,1)S(1)}, u32[]{:S(2)}, u32[]{:S(2)}) collective-permute-start(bf16[3,1,256,128]{3,2,1,0:T(8,128)(2,1)S(1)} %constant_dynamic-update-slice_fusion.9), channel_id=1, source_target_pairs={{0,1},{1,2},{2,3},{3,4},{4,5},{5,6},{6,7},{7,0},{8,9},{9,10},{10,1... | collective-permute-start | bytes 589832 | tf_op jit(solution)/shard_map/ppermute | solution.py:19
  23.3 10.6 %collective-permute-start.3 = (bf16[3,1,256,128]{3,2,1,0:T(8,128)(2,1)S(1)}, bf16[3,1,256,128]{3,2,1,0:T(8,128)(2,1)S(1)}, u32[]{:S(2)}, u32[]{:S(2)}) collective-permute-start(bf16[3,1,256,128]{3,2,1,0:T(8,128)(2,1)S(1)} %constant_dynamic-update-slice_fusion.9), channel_id=1, source_target_pairs={{1,0},{2,1},{3,2},{4,3},{5,4},{6,5},{7,6},{0,7},{9,8},{10,9},{11,1... | collective-permute-start | bytes 589832 | tf_op jit(solution)/shard_map/ppermute | solution.py:21
  49.9 2.0 copy-start.5
  51.9 3.6 %copy-start.3 = (f32[1,1,9,128,128]{4,3,2,1,0:T(8,128)S(1)}, f32[1,1,9,128,128]{4,3,2,1,0:T(8,128)}, u32[]{:S(2)}) copy-start(f32[1,1,9,128,128]{4,3,2,1,0:T(8,128)} %convert_element_type.43) | copy-start | bytes 1769476
  56.5 2.4 %copy-start.9 = (f32[32,128]{1,0:T(8,128)S(1)}, f32[32,128]{1,0:T(8,128)}, u32[]{:S(2)}) copy-start(f32[32,128]{1,0:T(8,128)} %copy-done.8) | copy-start | bytes 49156
  66.3 2.4 %copy-start.1 = (f32[32,128,128]{2,1,0:T(8,128)}, f32[32,128,128]{2,1,0:T(8,128)S(1)}, u32[]{:S(2)}) copy-start(f32[32,128,128]{2,1,0:T(8,128)S(1)} %multiply_reduce_fusion) | copy-start | bytes 6291460
  68.7 25.0 %copy-start.12 = (f32[16]{0:T(128)S(1)}, f32[16]{0:T(128)}, u32[]{:S(2)}) copy-start(f32[16]{0:T(128)} %copy-done.11) | copy-start | bytes 196
  91.7 2.1 copy-start.2
  91.8 10.7 %collective-permute-start.4 = (f32[1,3,256,128]{3,2,1,0:T(8,128)S(1)}, f32[1,3,256,128]{3,2,1,0:T(8,128)S(1)}, u32[]{:S(2)}, u32[]{:S(2)}) collective-permute-start(f32[1,3,256,128]{3,2,1,0:T(8,128)S(1)} %bitcast.174), channel_id=1, source_target_pairs={{0,8},{8,16},{16,24},{24,0},{1,9},{9,17},{17,25},{25,1},{2,10},{10... | collective-permute-start | bytes 1179656 | tf_op jit(solution)/shard_map/ppermute | solution.py:19
  91.8 10.6 %collective-permute-start.5 = (f32[1,3,256,128]{3,2,1,0:T(8,128)S(1)}, f32[1,3,256,128]{3,2,1,0:T(8,128)S(1)}, u32[]{:S(2)}, u32[]{:S(2)}) collective-permute-start(f32[1,3,256,128]{3,2,1,0:T(8,128)S(1)} %bitcast.173), channel_id=1, source_target_pairs={{8,0},{16,8},{24,16},{0,24},{9,1},{17,9},{25,17},{1,25},{10,2},{18... | collective-permute-start | bytes 1179656 | tf_op jit(solution)/shard_map/ppermute | solution.py:21
  95.1 12.9 %copy-start.10 = (f32[1,16,128]{2,1,0:T(8,128)S(1)}, f32[1,16,128]{2,1,0:T(8,128)}, u32[]{:S(2)}) copy-start(f32[1,16,128]{2,1,0:T(8,128)} %fusion.11) | copy-start | bytes 24580
  102.6 43.4 %collective-permute-start.6 = (f32[1,256,128]{2,1,0:T(8,128)S(1)}, f32[1,256,128]{2,1,0:T(8,128)S(1)}, u32[]{:S(2)}, u32[]{:S(2)}) collective-permute-start(f32[1,256,128]{2,1,0:T(8,128)S(1)} %get-tuple-element.16), channel_id=1, source_target_pairs={{0,1},{1,2},{2,3},{3,4},{4,5},{5,6},{6,7},{7,0},{8,9},{9,10},{10,1... | collective-permute-start | bytes 393224 | tf_op jit(solution)/shard_map/ppermute | solution.py:19
  102.9 43.1 %collective-permute-start.7 = (f32[1,256,128]{2,1,0:T(8,128)S(1)}, f32[1,256,128]{2,1,0:T(8,128)S(1)}, u32[]{:S(2)}, u32[]{:S(2)}) collective-permute-start(f32[1,256,128]{2,1,0:T(8,128)S(1)} %get-tuple-element.17), channel_id=1, source_target_pairs={{1,0},{2,1},{3,2},{4,3},{5,4},{6,5},{7,6},{0,7},{9,8},{10,9},{11,1... | collective-permute-start | bytes 393224 | tf_op jit(solution)/shard_map/ppermute | solution.py:21
Sparse Core Ops, SparseCore 0:
  108.2 120.2 all-reduce.1
where the time goes:
time: 238 us; the launch traced here: 237 us
  waiting for transfers between devices  96.5 us (41%)
  other arithmetic  45.1 us (19%)
  blocking collectives  37.9 us (16%)
  starting transfers between devices  14.7 us (6%)
  between operations  14.5 us (6%)
  matrix products  14.3 us (6%)
  local copies, waits for them, and re-layouts  14 us (6%)
    psum x1, waiting for transfers between devices, shards(): mix_total = lax.psum(mix_part, ('gz', 'xy'))  81.8 us
    psum x1, blocking collectives, shards(): radial_total = lax.psum(radial_part, ('gz', 'xy'))  37.9 us
    scatter-add x1, other arithmetic, shards(): grads = jnp.zeros((9 * natom, channels), jnp.float32).at[neighbour_local_...  22.9 us
    dot_general x4, matrix products, exact(): return jnp.einsum(form, left, right, precision=lax.Precision.HIGHEST)  12.7 us
    ppermute x4, waiting for transfers between devices, padded(): lax.ppermute(tail, axis, [(i, (i + 1) % count) for i in range(count)])  12.5 us
    gather x1, local copies, waits for them, and re-layouts, shards(): features = atom_table[neighbour_local_index].astype(jnp.float32)  12.1 us
    ppermute x4, starting transfers between devices, padded(): lax.ppermute(head, axis, [((i + 1) % count, i) for i in range(count)])  11.5 us
    reduce_sum x2, other arithmetic, shards(): jnp.sum(angular[span_start:span_end, :, :, None] * dmoment_float[span_sta...  5.34 us
  transfers between devices with their start and end apart: 9, of which 4 were waited for; matrix products, arithmetic and copies ran while one was open for 6% of the time, Pallas kernels for 0%

commit v1 on v0

v1 whole, which is shorter than its diff:
```python
import functools
import math

import jax
import jax.numpy as jnp
from jax import lax
from jax.experimental import pallas as pl
from jax.experimental.pallas import tpu as pltpu
from jax.sharding import PartitionSpec as P

CUTOFF = 4.0
LEVEL_SPANS = ((0, 1), (1, 4), (4, 9))
LEVEL_OF = (0, 1, 1, 1, 2, 2, 2, 2, 2)
ORDER = (0, 1, 2, 6, 7, 8, 3, 5, 4)
MESH = pl.DeviceIdType.MESH
TILE = 16
NT = (((1,), (1,)), ((), ()))
F32 = jnp.float32
BF16 = jnp.bfloat16


def dot(a, b):
    return jnp.dot(a, b, preferred_element_type=F32)


def dot_nt(a, b):
    return lax.dot_general(a, b, NT, preferred_element_type=F32)


def kernel(
    ngz, nxy,
    cot_ref, disp_ref, nbr_ref, cnt_ref, atom_ref, rw_ref, mw_ref,
    agrad_ref, rgrad_ref, mgrad_ref,
    tbl, oh, key, half, ang, dist, env, basis, wpad, wt, radial, feat, cott, mixt,
    mom, dmom, ft, con, gsend, grecv, mixp, mixrs, mixgz, radgz, radxy,
    halo_s, halo_r, back_s, back_r, mrs_s, mrs_r, mgz_s, mgz_r, mag_s, mag_r,
    rgz_s, rgz_r, rxy_s, rxy_r,
):
    g = lax.axis_index("gz")
    b = lax.axis_index("xy")
    nk, npr = nbr_ref.shape[2], nbr_ref.shape[3]
    ch = atom_ref.shape[3]
    hb = atom_ref.shape[2] // 2
    nb = rw_ref.shape[1]
    rows = ch // nxy

    def at(dg, db):
        return (lax.rem(g + dg + ngz, ngz), lax.rem(b + db + nxy, nxy))

    barrier = pltpu.get_barrier_semaphore()
    peers = [(0, d) for d in range(1, nxy)] + [(d, 0) for d in range(1, ngz)]
    peers += [(-1, -1), (-1, 1), (1, -1), (1, 1)]
    for dg, db in peers:
        pl.semaphore_signal(barrier, inc=1, device_id=at(dg, db), device_id_type=MESH)

    own = pl.ds(8 * hb, hb)
    for h in range(2):
        tbl[h * ch:(h + 1) * ch, own] = (
            atom_ref[0, 0, h * hb:(h + 1) * hb, :].astype(F32).T.astype(BF16)
        )
    pl.semaphore_wait(barrier, len(peers))

    halo = []
    for pos in range(8):
        s = ORDER[pos]
        dg, db = s // 3 - 1, s % 3 - 1
        halo.append(pltpu.make_async_remote_copy(
            src_ref=tbl.at[:, own], dst_ref=tbl.at[:, pl.ds(pos * hb, hb)],
            send_sem=halo_s.at[pos], recv_sem=halo_r.at[pos],
            device_id=at(-dg, -db), device_id_type=MESH))
    for c in halo:
        c.start()

    n = nbr_ref[0, 0]
    low = lax.bitwise_and(n, hb - 1)
    slot = lax.shift_right_logical(n, int(math.log2(2 * hb)))
    for pos in range(9):
        key[pos] = jnp.where(slot == ORDER[pos], low, -1).astype(F32)
    half[...] = lax.bitwise_and(n, hb)
    x = disp_ref[0, 0, 0] * (1.0 / CUTOFF)
    y = disp_ref[0, 0, 1] * (1.0 / CUTOFF)
    z = disp_ref[0, 0, 2] * (1.0 / CUTOFF)
    mask = (lax.broadcasted_iota(jnp.int32, (nk, npr), 0) < cnt_ref[0]).astype(F32)
    r3, r5, r15 = math.sqrt(3.0), math.sqrt(5.0), math.sqrt(15.0)
    comps = (
        None, r3 * x, r3 * y, r3 * z, r15 * x * y, r15 * y * z,
        0.5 * r5 * (2.0 * z * z - x * x - y * y), r15 * x * z, 0.5 * r15 * (x * x - y * y),
    )
    for m in range(9):
        ang[m] = mask if m == 0 else comps[m] * mask
    d0, d1, d2 = disp_ref[0, 0, 0], disp_ref[0, 0, 1], disp_ref[0, 0, 2]
    r = jnp.sqrt(d0 * d0 + d1 * d1 + d2 * d2)
    dist[...] = r
    env[...] = 0.5 * (jnp.cos(r * (math.pi / CUTOFF)) + 1.0)

    wpad[...] = jnp.zeros(wpad.shape, F32)
    for l in range(3):
        w = rw_ref[l]
        hi = w.astype(BF16).astype(F32)
        lanes = slice(l * ch, (l + 1) * ch)
        wpad[0:nb, lanes] = hi
        wpad[nb:2 * nb, lanes] = w - hi
        wpad[2 * nb:3 * nb, lanes] = hi
        wt[lanes, :] = wpad[:, lanes].T.astype(BF16)
        mixt[l] = mw_ref[l].astype(F32).T.astype(BF16)
    for m in range(9):
        cott[m] = cot_ref[0, 0, m].astype(F32).T

    step = CUTOFF / (nb - 1)
    sharp = ((nb - 1) / CUTOFF) ** 2
    centres = lax.broadcasted_iota(jnp.int32, (nb, npr), 0).astype(F32) * step
    lines = lax.broadcasted_iota(jnp.int32, (hb, npr), 0).astype(F32).astype(BF16)
    one = jnp.ones((hb, npr), BF16)
    zero = jnp.zeros((hb, npr), BF16)

    def lanes_of(k, count=1):
        return pl.ds(pl.multiple_of(k * npr, npr), count * npr)

    def prepare(c, carry):
        for j in range(2):
            k = c * 2 + j
            at_k = lanes_of(k)
            off = dist[pl.ds(k, 1), :] - centres
            shaped = jnp.exp(-sharp * (off * off)) * env[pl.ds(k, 1), :]
            hi = shaped.astype(BF16)
            basis[0:nb, at_k] = hi
            basis[nb:2 * nb, at_k] = hi
            basis[2 * nb:3 * nb, at_k] = (shaped - hi.astype(F32)).astype(BF16)
            for pos in range(9):
                row = jnp.broadcast_to(key[pos, pl.ds(k, 1), :], (hb, npr)).astype(BF16)
                oh[pos * hb:(pos + 1) * hb, at_k] = jnp.where(lines == row, one, zero)
        rad = dot(wt[:, 0:3 * nb], basis[:, lanes_of(c * 2, 2)])
        for j in range(2):
            radial[c * 2 + j] = rad[:, j * npr:(j + 1) * npr]
        return carry

    lax.fori_loop(0, nk // 2, prepare, 0)

    for c in halo:
        c.wait_recv()

    def gather(c, carry):
        both = dot(tbl[...], oh[:, lanes_of(c * 2, 2)])
        for j in range(2):
            k = c * 2 + j
            cols = slice(j * npr, (j + 1) * npr)
            upper = half[pl.ds(k, 1), :] > 0
            feat[k] = jnp.where(upper, both[ch:, cols], both[:ch, cols])
        return carry

    lax.fori_loop(0, nk // 2, gather, 0)

    def moment_tile(t, carry):
        at_t = pl.ds(pl.multiple_of(t * TILE, TILE), TILE)

        def body(k, acc):
            f = feat[k, at_t, :]
            w = [
                radial[k, pl.ds(pl.multiple_of(l * ch + t * TILE, TILE), TILE), :] * f
                for l in range(3)
            ]
            return tuple(
                acc[m] + ang[m, pl.ds(k, 1), :] * w[LEVEL_OF[m]] for m in range(9)
            )

        acc = lax.fori_loop(0, nk, body, tuple(jnp.zeros((TILE, npr), F32) for _ in range(9)),
                            unroll=4)
        for m in range(9):
            mom[at_t, m * npr:(m + 1) * npr] = acc[m].astype(BF16)
        return carry

    lax.fori_loop(0, ch // TILE, moment_tile, 0)

    scalar = dot(mixt[0], mom[:, 0:npr])
    gating = jax.nn.sigmoid(scalar)
    slope = gating * (1.0 - gating)
    inner = jnp.zeros((ch, npr), F32)
    dmx = [None] * 9
    for m in range(1, 9):
        inner = inner + cott[m] * dot(mixt[LEVEL_OF[m]], mom[:, m * npr:(m + 1) * npr])
        dmx[m] = (cott[m] * gating).astype(BF16)
    dmx[0] = (cott[0] * (gating + scalar * slope) + inner * slope).astype(BF16)
    for l, (lo, hi) in enumerate(LEVEL_SPANS):
        total = None
        for m in range(lo, hi):
            part = dot_nt(mom[:, m * npr:(m + 1) * npr], dmx[m])
            total = part if total is None else total + part
        mixp[l] = total

    mixrs[b] = mixp[:, pl.ds(pl.multiple_of(b * rows, rows), rows), :]
    mrs = []
    for d in range(1, nxy):
        to = lax.rem(b + d, nxy)
        mrs.append(pltpu.make_async_remote_copy(
            src_ref=mixp.at[:, pl.ds(pl.multiple_of(to * rows, rows), rows), :],
            dst_ref=mixrs.at[b],
            send_sem=mrs_s.at[d], recv_sem=mrs_r.at[d],
            device_id=(g, to), device_id_type=MESH))
    for c in mrs:
        c.start()

    for m in range(9):
        dmom[m] = dot(mw_ref[LEVEL_OF[m]], dmx[m]).astype(BF16).astype(F32)

    def trace_tile(t, carry):
        at_t = pl.ds(pl.multiple_of(t * TILE, TILE), TILE)
        dm = [dmom[m, at_t, :] for m in range(9)]

        def body(k, carry):
            f = feat[k, at_t, :]
            at_k = lanes_of(k)
            total = None
            for l, (lo, hi) in enumerate(LEVEL_SPANS):
                tr = None
                for m in range(lo, hi):
                    part = ang[m, pl.ds(k, 1), :] * dm[m]
                    tr = part if tr is None else tr + part
                at_l = pl.ds(pl.multiple_of(l * ch + t * TILE, TILE), TILE)
                part = radial[k, at_l, :] * tr
                total = part if total is None else total + part
                ft[at_l, at_k] = (f * tr).astype(BF16)
            upper = half[pl.ds(k, 1), :] > 0
            con[at_t, at_k] = jnp.where(upper, 0.0, total).astype(BF16)
            con[pl.ds(pl.multiple_of(ch + t * TILE, TILE), TILE), at_k] = (
                jnp.where(upper, total, 0.0).astype(BF16)
            )
            return carry

        return lax.fori_loop(0, nk, body, carry, unroll=4)

    lax.fori_loop(0, ch // TILE, trace_tile, 0)

    rad = dot_nt(basis[...], ft[...])
    rad = rad[0:nb] + rad[2 * nb:3 * nb]
    for l in range(3):
        radgz[g, l] = rad[:, l * ch:(l + 1) * ch]
    rgz = []
    for d in range(1, ngz):
        rgz.append(pltpu.make_async_remote_copy(
            src_ref=radgz.at[g], dst_ref=radgz.at[g],
            send_sem=rgz_s.at[d], recv_sem=rgz_r.at[d],
            device_id=at(d, 0), device_id_type=MESH))
    for c in rgz:
        c.start()

    for c in mrs:
        c.wait_recv()
    total = mixrs[0]
    for i in range(1, nxy):
        total = total + mixrs[i]
    mixgz[g] = total
    mgz = []
    for d in range(1, ngz):
        mgz.append(pltpu.make_async_remote_copy(
            src_ref=mixgz.at[g], dst_ref=mixgz.at[g],
            send_sem=mgz_s.at[d], recv_sem=mgz_r.at[d],
            device_id=at(d, 0), device_id_type=MESH))
    for c in mgz:
        c.start()

    back = []

    def scatter(first, last):
        res = dot_nt(oh[first * hb:last * hb, :], con[...])
        for pos in range(first, last):
            block = res[(pos - first) * hb:(pos - first + 1) * hb]
            gsend[pos, 0:hb] = block[:, :ch].astype(BF16)
            gsend[pos, hb:2 * hb] = block[:, ch:].astype(BF16)
            s = ORDER[pos]
            copy = pltpu.make_async_remote_copy(
                src_ref=gsend.at[pos], dst_ref=grecv.at[pos],
                send_sem=back_s.at[pos], recv_sem=back_r.at[pos],
                device_id=at(s // 3 - 1, s % 3 - 1), device_id_type=MESH)
            copy.start()
            back.append(copy)

    scatter(0, 3)

    for c in rgz:
        c.wait_recv()
    total = radgz[0]
    for i in range(1, ngz):
        total = total + radgz[i]
    radxy[b] = total
    rxy = []
    for d in range(1, nxy):
        rxy.append(pltpu.make_async_remote_copy(
            src_ref=radxy.at[b], dst_ref=radxy.at[b],
            send_sem=rxy_s.at[d], recv_sem=rxy_r.at[d],
            device_id=at(0, d), device_id_type=MESH))
    for c in rxy:
        c.start()

    scatter(3, 6)

    for c in mgz:
        c.wait_recv()
    total = mixgz[0]
    for i in range(1, ngz):
        total = total + mixgz[i]
    mine = pl.ds(pl.multiple_of(b * rows, rows), rows)
    mgrad_ref[:, mine, :] = total
    mag = []
    for d in range(1, nxy):
        mag.append(pltpu.make_async_remote_copy(
            src_ref=mgrad_ref.at[:, mine, :], dst_ref=mgrad_ref.at[:, mine, :],
            send_sem=mag_s.at[d], recv_sem=mag_r.at[d],
            device_id=at(0, d), device_id_type=MESH))
    for c in mag:
        c.start()

    scatter(6, 8)
    kept = dot_nt(oh[8 * hb:9 * hb, :], con[...])
    agrad_ref[0, 0, 0:hb] = kept[:, :ch]
    agrad_ref[0, 0, hb:2 * hb] = kept[:, ch:]

    for c in rxy:
        c.wait_recv()
    total = radxy[0]
    for i in range(1, nxy):
        total = total + radxy[i]
    rgrad_ref[...] = total

    for c in back:
        c.wait_recv()
    for h in range(2):
        part = agrad_ref[0, 0, h * hb:(h + 1) * hb]
        for pos in range(8):
            part = part + grecv[pos, h * hb:(h + 1) * hb].astype(F32)
        agrad_ref[0, 0, h * hb:(h + 1) * hb] = part
    for c in mag:
        c.wait_recv()
    for c in halo + mrs + rgz + mgz + back + rxy + mag:
        c.wait_send()


def shards(cotangent, displacement, neighbours, counts, atom_feat, radial_weight, mix_weight):
    ngz, nxy = lax.axis_size("gz"), lax.axis_size("xy")
    nk, npr = neighbours.shape[2:]
    natom, ch = atom_feat.shape[2:]
    nb = radial_weight.shape[1]
    hb = natom // 2
    slots = nk * npr
    rows = ch // nxy
    V = pltpu.VMEM
    dma = pltpu.SemaphoreType.DMA
    vm = pl.BlockSpec(memory_space=pltpu.VMEM)
    return pl.pallas_call(
        functools.partial(kernel, ngz, nxy),
        out_shape=(
            jax.ShapeDtypeStruct((1, 1, natom, ch), F32),
            jax.ShapeDtypeStruct((3, nb, ch), F32),
            jax.ShapeDtypeStruct((3, ch, ch), F32),
        ),
        in_specs=[vm] * 7,
        out_specs=(vm, vm, vm),
        scratch_shapes=[
            V((2 * ch, 9 * hb), BF16),
            V((9 * hb, slots), BF16),
            V((9, nk, npr), F32),
            V((nk, npr), jnp.int32),
            V((9, nk, npr), F32),
            V((nk, npr), F32),
            V((nk, npr), F32),
            V((3 * nb, slots), BF16),
            V((128, 3 * ch), F32),
            V((3 * ch, 128), BF16),
            V((nk, 3 * ch, npr), F32),
            V((nk, ch, npr), F32),
            V((9, ch, npr), F32),
            V((3, ch, ch), BF16),
            V((ch, 9 * npr), BF16),
            V((9, ch, npr), F32),
            V((3 * ch, slots), BF16),
            V((2 * ch, slots), BF16),
            V((8, natom, ch), BF16),
            V((8, natom, ch), BF16),
            V((3, ch, ch), F32),
            V((nxy, 3, rows, ch), F32),
            V((ngz, 3, rows, ch), F32),
            V((ngz, 3, nb, ch), F32),
            V((nxy, 3, nb, ch), F32),
            dma((8,)), dma((8,)), dma((8,)), dma((8,)),
            dma((nxy,)), dma((nxy,)), dma((ngz,)), dma((ngz,)), dma((nxy,)), dma((nxy,)),
            dma((ngz,)), dma((ngz,)), dma((nxy,)), dma((nxy,)),
        ],
        compiler_params=pltpu.CompilerParams(
            collective_id=0, has_side_effects=True, vmem_limit_bytes=48 * 1024 * 1024
        ),
    )(cotangent, displacement, neighbours, counts, atom_feat, radial_weight, mix_weight)


def solution(mesh):
    in_specs = (
        P("gz", "xy", None, None, None),
        P("gz", "xy", None, None, None),
        P("gz", "xy", None, None),
        P("gz", "xy", None),
        P("gz", "xy", None, None),
        P(),
        P(),
    )
    out_specs = (P("gz", "xy", None, None), P(), P())
    return jax.shard_map(shards, mesh=mesh, in_specs=in_specs, out_specs=out_specs, check_vma=False)
```

time: 238 us -> 55.6 us (0.23)
  waiting for transfers between devices: 96.5 us -> 0 us
  Pallas kernels: 0 us -> 47 us
  other arithmetic: 45.1 us -> 0 us
  blocking collectives: 37.9 us -> 0 us
  starting transfers between devices: 14.7 us -> 0 us
  matrix products: 14.3 us -> 0 us
  between operations: 14.5 us -> 0.66 us
  local copies, waits for them, and re-layouts: 14 us -> 7.53 us
    psum x1 -> x0, waiting for transfers between devices: 81.8 us -> none  [shards(): mix_total = lax.psum(mix_part, ('gz', 'xy'))]
    pallas_call x0 -> x1, Pallas kernels: none -> 47 us  [shards(): pl.pallas_call(functools.partial(kernel, ngz, nxy), out_shape=(jax.ShapeD...]
    psum x1 -> x0, blocking collectives: 37.9 us -> none  [shards(): radial_total = lax.psum(radial_part, ('gz', 'xy'))]
    scatter-add x1 -> x0, other arithmetic: 22.9 us -> none  [shards(): grads = jnp.zeros((9 * natom, channels), jnp.float32).at[neighbour_local_...]
    ppermute x8 -> x0, waiting for transfers between devices: 14.7 us -> none  [the longest x4 12.5 us: padded(): lax.ppermute(tail, axis, [(i, (i + 1) % count) for i in range(count)])]
    ppermute x8 -> x0, starting transfers between devices: 14.6 us -> none  [the longest x4 11.5 us: padded(): lax.ppermute(head, axis, [((i + 1) % count, i) for i in range(count)])]
    dot_general x13 -> x0, matrix products: 14.3 us -> none  [the longest x4 12.7 us: exact(): return jnp.einsum(form, left, right, precision=lax.Precision.HIGHEST)]
    gather x1 -> x0, local copies, waits for them, and re-layouts: 12.1 us -> none  [shards(): features = atom_table[neighbour_local_index].astype(jnp.float32)]
  transfers between devices with their start and end apart: 9 -> 0, of which waited for: 4 -> 0; matrix products, arithmetic and copies ran while one was open for 6% -> 0% of each run, Pallas kernels for 0% -> 0%
where the time goes in v1:
time: 55.6 us; the launch traced here: 55.2 us
  Pallas kernels  47 us (85%)
  local copies, waits for them, and re-layouts  7.53 us (14%)
  between operations  0.66 us (1%)
    pallas_call x1, Pallas kernels, shards(): pl.pallas_call(functools.partial(kernel, ngz, nxy), out_shape=(jax.ShapeD...  47 us
    unnamed x17, local copies, waits for them, and re-layouts  7.53 us

profile of v1, /device:TPU:0, one launch (start us, length us, event | category | flops | bytes accessed | tf_op | source)
XLA Modules:
  0.0 55.2 jit_solution(18373760034659324532)
XLA Ops:
  0.6 0.0 copy-start
  0.6 1.0 %copy-done = bf16[1,1,9,128,128]{4,3,2,1,0:T(8,128)(2,1)S(1)} copy-done((bf16[1,1,9,128,128]{4,3,2,1,0:T(8,128)(2,1)S(1)}, bf16[1,1,9,128,128]{4,3,2,1,0:T(8,128)(2,1)}, u32[]{:S(2)}) %copy-start) | copy-done | bytes 294936
  1.6 0.0 copy-start.1
  1.6 0.9 %copy-done.1 = bf16[3,128,128]{2,1,0:T(8,128)(2,1)S(1)} copy-done((bf16[3,128,128]{2,1,0:T(8,128)(2,1)S(1)}, bf16[3,128,128]{2,1,0:T(8,128)(2,1)}, u32[]{:S(2)}) %copy-start.1) | copy-done | bytes 98328
  2.5 0.0 copy-start.2
  2.5 0.8 %copy-done.2 = bf16[1,1,256,128]{3,2,1,0:T(8,128)(2,1)S(1)} copy-done((bf16[1,1,256,128]{3,2,1,0:T(8,128)(2,1)S(1)}, bf16[1,1,256,128]{3,2,1,0:T(8,128)(2,1)}, u32[]{:S(2)}) %copy-start.2) | copy-done | bytes 65560
  3.3 0.0 copy-start.3
  3.3 0.8 %copy-done.3 = f32[1,1,3,32,128]{4,3,2,1,0:T(8,128)S(1)} copy-done((f32[1,1,3,32,128]{4,3,2,1,0:T(8,128)S(1)}, f32[1,1,3,32,128]{4,3,2,1,0:T(8,128)}, u32[]{:S(2)}) %copy-start.3) | copy-done | bytes 49176
  4.1 0.0 copy-start.4
  4.1 0.7 %copy-done.4 = f32[3,16,128]{2,1,0:T(8,128)S(1)} copy-done((f32[3,16,128]{2,1,0:T(8,128)S(1)}, f32[3,16,128]{2,1,0:T(8,128)}, u32[]{:S(2)}) %copy-start.4) | copy-done | bytes 24600
  4.9 0.0 copy-start.5
  4.9 0.7 %copy-done.5 = s32[1,1,32,128]{3,2,1,0:T(8,128)S(1)} copy-done((s32[1,1,32,128]{3,2,1,0:T(8,128)S(1)}, s32[1,1,32,128]{3,2,1,0:T(8,128)}, u32[]{:S(2)}) %copy-start.5) | copy-done | bytes 16408
  5.6 0.0 copy-start.6
  5.6 0.7 %copy-done.6 = s32[1,1,128]{2,1,0:T(1,128)S(1)} copy-done((s32[1,1,128]{2,1,0:T(1,128)S(1)}, s32[1,1,128]{2,1,0:T(1,128)}, u32[]{:S(2)}) %copy-start.6) | copy-done | bytes 536
  6.2 47.0 %shard_map.94 = (f32[1,1,256,128]{3,2,1,0:T(8,128)S(1)}, f32[3,16,128]{2,1,0:T(8,128)S(1)}, f32[3,128,128]{2,1,0:T(8,128)S(1)}) custom-call(bf16[1,1,9,128,128]{4,3,2,1,0:T(8,128)(2,1)S(1)} %copy-done, f32[1,1,3,32,128]{4,3,2,1,0:T(8,128)S(1)} %copy-done.3, s32[1,1,32,128]{3,2,1,0:T(8,128)S(1)} %copy-done.5, s32[1,1,128]{2,1,0:T(1,128)S(1)} %copy-done.6, ...), custom_call_target="tpu_custom_call" | custom-call | tf_op jit(solution)/shard_map/pallas_call | solution.py:348
  53.3 0.7 %copy.13 = f32[1,1,256,128]{3,2,1,0:T(8,128)} copy(f32[1,1,256,128]{3,2,1,0:T(8,128)S(1)} %get-tuple-element.6) | data formatting | bytes 262144
  53.9 0.6 %copy.14 = f32[3,16,128]{2,1,0:T(8,128)} copy(f32[3,16,128]{2,1,0:T(8,128)S(1)} %get-tuple-element.7) | data formatting | bytes 49152
  54.6 0.7 %copy.15 = f32[3,128,128]{2,1,0:T(8,128)} copy(f32[3,128,128]{2,1,0:T(8,128)S(1)} %get-tuple-element.8) | data formatting | bytes 393216
Async XLA Ops:
  0.6 1.0 %copy-start = (bf16[1,1,9,128,128]{4,3,2,1,0:T(8,128)(2,1)S(1)}, bf16[1,1,9,128,128]{4,3,2,1,0:T(8,128)(2,1)}, u32[]{:S(2)}) copy-start(bf16[1,1,9,128,128]{4,3,2,1,0:T(8,128)(2,1)} %cot_ref.1) | copy-start | bytes 884740
  1.6 0.9 %copy-start.1 = (bf16[3,128,128]{2,1,0:T(8,128)(2,1)S(1)}, bf16[3,128,128]{2,1,0:T(8,128)(2,1)}, u32[]{:S(2)}) copy-start(bf16[3,128,128]{2,1,0:T(8,128)(2,1)} %mw_ref.1) | copy-start | bytes 294916
  2.5 0.8 %copy-start.2 = (bf16[1,1,256,128]{3,2,1,0:T(8,128)(2,1)S(1)}, bf16[1,1,256,128]{3,2,1,0:T(8,128)(2,1)}, u32[]{:S(2)}) copy-start(bf16[1,1,256,128]{3,2,1,0:T(8,128)(2,1)} %atom_ref.1) | copy-start | bytes 196612
  3.3 0.8 %copy-start.3 = (f32[1,1,3,32,128]{4,3,2,1,0:T(8,128)S(1)}, f32[1,1,3,32,128]{4,3,2,1,0:T(8,128)}, u32[]{:S(2)}) copy-start(f32[1,1,3,32,128]{4,3,2,1,0:T(8,128)} %disp_ref.1) | copy-start | bytes 147460
  4.1 0.7 %copy-start.4 = (f32[3,16,128]{2,1,0:T(8,128)S(1)}, f32[3,16,128]{2,1,0:T(8,128)}, u32[]{:S(2)}) copy-start(f32[3,16,128]{2,1,0:T(8,128)} %rw_ref.1) | copy-start | bytes 73732
  4.9 0.7 %copy-start.5 = (s32[1,1,32,128]{3,2,1,0:T(8,128)S(1)}, s32[1,1,32,128]{3,2,1,0:T(8,128)}, u32[]{:S(2)}) copy-start(s32[1,1,32,128]{3,2,1,0:T(8,128)} %nbr_ref.1) | copy-start | bytes 49156
  5.6 0.7 %copy-start.6 = (s32[1,1,128]{2,1,0:T(1,128)S(1)}, s32[1,1,128]{2,1,0:T(1,128)}, u32[]{:S(2)}) copy-start(s32[1,1,128]{2,1,0:T(1,128)} %cnt_ref.1) | copy-start | bytes 1540

commit v2 on v1

--- a/solution.py
+++ b/solution.py
@@ -27,14 +27,22 @@
     return lax.dot_general(a, b, NT, preferred_element_type=F32)
 
 
+def added(ref):
+    total = ref[0].astype(F32)
+    for i in range(1, ref.shape[0]):
+        total = total + ref[i].astype(F32)
+    return total
+
+
 def kernel(
     ngz, nxy,
-    cot_ref, disp_ref, nbr_ref, cnt_ref, atom_ref, rw_ref, mw_ref,
+    cot_hbm, disp_hbm, nbr_hbm, cnt_hbm, atom_hbm, rw_hbm, mw_hbm,
     agrad_ref, rgrad_ref, mgrad_ref,
     tbl, oh, key, half, ang, dist, env, basis, wpad, wt, radial, feat, cott, mixt,
-    mom, dmom, ft, con, gsend, grecv, mixp, mixrs, mixgz, radgz, radxy,
+    mom, dmom, ft, con, gsend, grecv, mixp, mixrs, mixgz, mixag, radgz, radxy,
     halo_s, halo_r, back_s, back_r, mrs_s, mrs_r, mgz_s, mgz_r, mag_s, mag_r,
     rgz_s, rgz_r, rxy_s, rxy_r,
+    atom_ref, nbr_ref, disp_ref, cnt_ref, rw_ref, mw_ref, cot_ref, load_s,
 ):
     g = lax.axis_index("gz")
     b = lax.axis_index("xy")
@@ -47,6 +55,16 @@
     def at(dg, db):
         return (lax.rem(g + dg + ngz, ngz), lax.rem(b + db + nxy, nxy))
 
+    loads = [
+        pltpu.make_async_copy(src, dst, load_s.at[i])
+        for i, (src, dst) in enumerate((
+            (atom_hbm, atom_ref), (nbr_hbm, nbr_ref), (disp_hbm, disp_ref), (cnt_hbm, cnt_ref),
+            (rw_hbm, rw_ref), (mw_hbm, mw_ref), (cot_hbm, cot_ref),
+        ))
+    ]
+    for c in loads:
+        c.start()
+
     barrier = pltpu.get_barrier_semaphore()
     peers = [(0, d) for d in range(1, nxy)] + [(d, 0) for d in range(1, ngz)]
     peers += [(-1, -1), (-1, 1), (1, -1), (1, 1)]
@@ -54,6 +72,7 @@
         pl.semaphore_signal(barrier, inc=1, device_id=at(dg, db), device_id_type=MESH)
 
     own = pl.ds(8 * hb, hb)
+    loads[0].wait()
     for h in range(2):
         tbl[h * ch:(h + 1) * ch, own] = (
             atom_ref[0, 0, h * hb:(h + 1) * hb, :].astype(F32).T.astype(BF16)
@@ -71,6 +90,8 @@
     for c in halo:
         c.start()
 
+    for c in loads[1:]:
+        c.wait()
     n = nbr_ref[0, 0]
     low = lax.bitwise_and(n, hb - 1)
     slot = lax.shift_right_logical(n, int(math.log2(2 * hb)))
@@ -185,14 +206,15 @@
         for m in range(lo, hi):
             part = dot_nt(mom[:, m * npr:(m + 1) * npr], dmx[m])
             total = part if total is None else total + part
-        mixp[l] = total
-
-    mixrs[b] = mixp[:, pl.ds(pl.multiple_of(b * rows, rows), rows), :]
+        for i in range(nxy):
+            mixp[i, l] = total[i * rows:(i + 1) * rows].astype(mixp.dtype)
+
+    mixrs[b] = mixp[b]
     mrs = []
     for d in range(1, nxy):
         to = lax.rem(b + d, nxy)
         mrs.append(pltpu.make_async_remote_copy(
-            src_ref=mixp.at[:, pl.ds(pl.multiple_of(to * rows, rows), rows), :],
+            src_ref=mixp.at[to],
             dst_ref=mixrs.at[b],
             send_sem=mrs_s.at[d], recv_sem=mrs_r.at[d],
             device_id=(g, to), device_id_type=MESH))
@@ -233,7 +255,7 @@
     rad = dot_nt(basis[...], ft[...])
     rad = rad[0:nb] + rad[2 * nb:3 * nb]
     for l in range(3):
-        radgz[g, l] = rad[:, l * ch:(l + 1) * ch]
+        radgz[g, l] = rad[:, l * ch:(l + 1) * ch].astype(BF16)
     rgz = []
     for d in range(1, ngz):
         rgz.append(pltpu.make_async_remote_copy(
@@ -245,10 +267,7 @@
 
     for c in mrs:
         c.wait_recv()
-    total = mixrs[0]
-    for i in range(1, nxy):
-        total = total + mixrs[i]
-    mixgz[g] = total
+    mixgz[g] = added(mixrs).astype(mixgz.dtype)
     mgz = []
     for d in range(1, ngz):
         mgz.append(pltpu.make_async_remote_copy(
@@ -278,10 +297,7 @@
 
     for c in rgz:
         c.wait_recv()
-    total = radgz[0]
-    for i in range(1, ngz):
-        total = total + radgz[i]
-    radxy[b] = total
+    radxy[b] = added(radgz).astype(BF16)
     rxy = []
     for d in range(1, nxy):
         rxy.append(pltpu.make_async_remote_copy(
@@ -295,15 +311,11 @@
 
     for c in mgz:
         c.wait_recv()
-    total = mixgz[0]
-    for i in range(1, ngz):
-        total = total + mixgz[i]
-    mine = pl.ds(pl.multiple_of(b * rows, rows), rows)
-    mgrad_ref[:, mine, :] = total
+    mixag[b] = added(mixgz).astype(mixag.dtype)
     mag = []
     for d in range(1, nxy):
         mag.append(pltpu.make_async_remote_copy(
-            src_ref=mgrad_ref.at[:, mine, :], dst_ref=mgrad_ref.at[:, mine, :],
+            src_ref=mixag.at[b], dst_ref=mixag.at[b],
             send_sem=mag_s.at[d], recv_sem=mag_r.at[d],
             device_id=at(0, d), device_id_type=MESH))
     for c in mag:
@@ -316,10 +328,7 @@
 
     for c in rxy:
         c.wait_recv()
-    total = radxy[0]
-    for i in range(1, nxy):
-        total = total + radxy[i]
-    rgrad_ref[...] = total
+    rgrad_ref[...] = added(radxy)
 
     for c in back:
         c.wait_recv()
@@ -330,6 +339,8 @@
         agrad_ref[0, 0, h * hb:(h + 1) * hb] = part
     for c in mag:
         c.wait_recv()
+    for i in range(nxy):
+        mgrad_ref[:, i * rows:(i + 1) * rows, :] = mixag[i].astype(F32)
     for c in halo + mrs + rgz + mgz + back + rxy + mag:
         c.wait_send()
 
@@ -342,6 +353,7 @@
     hb = natom // 2
     slots = nk * npr
     rows = ch // nxy
+    sent = F32 if rows % 16 else BF16
     V = pltpu.VMEM
     dma = pltpu.SemaphoreType.DMA
     vm = pl.BlockSpec(memory_space=pltpu.VMEM)
@@ -352,7 +364,7 @@
             jax.ShapeDtypeStruct((3, nb, ch), F32),
             jax.ShapeDtypeStruct((3, ch, ch), F32),
         ),
-        in_specs=[vm] * 7,
+        in_specs=[pl.BlockSpec(memory_space=pl.ANY)] * 7,
         out_specs=(vm, vm, vm),
         scratch_shapes=[
             V((2 * ch, 9 * hb), BF16),
@@ -375,14 +387,18 @@
             V((2 * ch, slots), BF16),
             V((8, natom, ch), BF16),
             V((8, natom, ch), BF16),
-            V((3, ch, ch), F32),
-            V((nxy, 3, rows, ch), F32),
-            V((ngz, 3, rows, ch), F32),
-            V((ngz, 3, nb, ch), F32),
-            V((nxy, 3, nb, ch), F32),
+            V((nxy, 3, rows, ch), sent),
+            V((nxy, 3, rows, ch), sent),
+            V((ngz, 3, rows, ch), sent),
+            V((nxy, 3, rows, ch), sent),
+            V((ngz, 3, nb, ch), BF16),
+            V((nxy, 3, nb, ch), BF16),
             dma((8,)), dma((8,)), dma((8,)), dma((8,)),
             dma((nxy,)), dma((nxy,)), dma((ngz,)), dma((ngz,)), dma((nxy,)), dma((nxy,)),
             dma((ngz,)), dma((ngz,)), dma((nxy,)), dma((nxy,)),
+            V(atom_feat.shape, BF16), V(neighbours.shape, jnp.int32), V(displacement.shape, F32),
+            V(counts.shape, jnp.int32), V(radial_weight.shape, F32), V(mix_weight.shape, BF16),
+            V(cotangent.shape, BF16), dma((7,)),
         ],
         compiler_params=pltpu.CompilerParams(
             collective_id=0, has_side_effects=True, vmem_limit_bytes=48 * 1024 * 1024

time: 55.6 us -> 52.7 us (0.948)
  Pallas kernels: 47 us -> 44.1 us
    pallas_call x1, Pallas kernels: 47 us -> 44.1 us  [shards(): pl.pallas_call(functools.partial(kernel, ngz, nxy), out_shape=(jax.ShapeD...]
where the time goes in v2:
time: 52.7 us; the launch traced here: 52.3 us
  Pallas kernels  44.1 us (84%)
  local copies, waits for them, and re-layouts  7.53 us (14%)
  between operations  0.66 us (1%)
    pallas_call x1, Pallas kernels, shards(): pl.pallas_call(functools.partial(kernel, ngz, nxy), out_shape=(jax.ShapeD...  44.1 us
    unnamed x17, local copies, waits for them, and re-layouts  7.53 us

profile of v2, /device:TPU:0, one launch (start us, length us, event | category | flops | bytes accessed | tf_op | source)
XLA Modules:
  0.0 52.3 jit_solution(17746580252641206982)
XLA Ops:
  0.6 0.0 copy-start
  0.6 1.0 %copy-done = bf16[1,1,9,128,128]{4,3,2,1,0:T(8,128)(2,1)S(1)} copy-done((bf16[1,1,9,128,128]{4,3,2,1,0:T(8,128)(2,1)S(1)}, bf16[1,1,9,128,128]{4,3,2,1,0:T(8,128)(2,1)}, u32[]{:S(2)}) %copy-start) | copy-done | bytes 294936
  1.6 0.0 copy-start.1
  1.6 0.9 %copy-done.1 = bf16[3,128,128]{2,1,0:T(8,128)(2,1)S(1)} copy-done((bf16[3,128,128]{2,1,0:T(8,128)(2,1)S(1)}, bf16[3,128,128]{2,1,0:T(8,128)(2,1)}, u32[]{:S(2)}) %copy-start.1) | copy-done | bytes 98328
  2.5 0.0 copy-start.2
  2.5 0.8 %copy-done.2 = bf16[1,1,256,128]{3,2,1,0:T(8,128)(2,1)S(1)} copy-done((bf16[1,1,256,128]{3,2,1,0:T(8,128)(2,1)S(1)}, bf16[1,1,256,128]{3,2,1,0:T(8,128)(2,1)}, u32[]{:S(2)}) %copy-start.2) | copy-done | bytes 65560
  3.3 0.0 copy-start.3
  3.3 0.8 %copy-done.3 = f32[1,1,3,32,128]{4,3,2,1,0:T(8,128)S(1)} copy-done((f32[1,1,3,32,128]{4,3,2,1,0:T(8,128)S(1)}, f32[1,1,3,32,128]{4,3,2,1,0:T(8,128)}, u32[]{:S(2)}) %copy-start.3) | copy-done | bytes 49176
  4.1 0.0 copy-start.4
  4.1 0.7 %copy-done.4 = f32[3,16,128]{2,1,0:T(8,128)S(1)} copy-done((f32[3,16,128]{2,1,0:T(8,128)S(1)}, f32[3,16,128]{2,1,0:T(8,128)}, u32[]{:S(2)}) %copy-start.4) | copy-done | bytes 24600
  4.9 0.0 copy-start.5
  4.9 0.7 %copy-done.5 = s32[1,1,32,128]{3,2,1,0:T(8,128)S(1)} copy-done((s32[1,1,32,128]{3,2,1,0:T(8,128)S(1)}, s32[1,1,32,128]{3,2,1,0:T(8,128)}, u32[]{:S(2)}) %copy-start.5) | copy-done | bytes 16408
  5.6 0.0 copy-start.6
  5.6 0.7 %copy-done.6 = s32[1,1,128]{2,1,0:T(1,128)S(1)} copy-done((s32[1,1,128]{2,1,0:T(1,128)S(1)}, s32[1,1,128]{2,1,0:T(1,128)}, u32[]{:S(2)}) %copy-start.6) | copy-done | bytes 536
  6.2 44.1 %shard_map.94 = (f32[1,1,256,128]{3,2,1,0:T(8,128)S(1)}, f32[3,16,128]{2,1,0:T(8,128)S(1)}, f32[3,128,128]{2,1,0:T(8,128)S(1)}) custom-call(bf16[1,1,9,128,128]{4,3,2,1,0:T(8,128)(2,1)S(1)} %copy-done, f32[1,1,3,32,128]{4,3,2,1,0:T(8,128)S(1)} %copy-done.3, s32[1,1,32,128]{3,2,1,0:T(8,128)S(1)} %copy-done.5, s32[1,1,128]{2,1,0:T(1,128)S(1)} %copy-done.6, ...), custom_call_target="tpu_custom_call" | custom-call | tf_op jit(solution)/shard_map/pallas_call | solution.py:360
  50.3 0.7 %copy.13 = f32[1,1,256,128]{3,2,1,0:T(8,128)} copy(f32[1,1,256,128]{3,2,1,0:T(8,128)S(1)} %get-tuple-element.6) | data formatting | bytes 262144
  51.0 0.6 %copy.14 = f32[3,16,128]{2,1,0:T(8,128)} copy(f32[3,16,128]{2,1,0:T(8,128)S(1)} %get-tuple-element.7) | data formatting | bytes 49152
  51.6 0.7 %copy.15 = f32[3,128,128]{2,1,0:T(8,128)} copy(f32[3,128,128]{2,1,0:T(8,128)S(1)} %get-tuple-element.8) | data formatting | bytes 393216
Async XLA Ops:
  0.6 1.0 %copy-start = (bf16[1,1,9,128,128]{4,3,2,1,0:T(8,128)(2,1)S(1)}, bf16[1,1,9,128,128]{4,3,2,1,0:T(8,128)(2,1)}, u32[]{:S(2)}) copy-start(bf16[1,1,9,128,128]{4,3,2,1,0:T(8,128)(2,1)} %cot_hbm.1) | copy-start | bytes 884740
  1.6 0.9 %copy-start.1 = (bf16[3,128,128]{2,1,0:T(8,128)(2,1)S(1)}, bf16[3,128,128]{2,1,0:T(8,128)(2,1)}, u32[]{:S(2)}) copy-start(bf16[3,128,128]{2,1,0:T(8,128)(2,1)} %mw_hbm.1) | copy-start | bytes 294916
  2.5 0.8 %copy-start.2 = (bf16[1,1,256,128]{3,2,1,0:T(8,128)(2,1)S(1)}, bf16[1,1,256,128]{3,2,1,0:T(8,128)(2,1)}, u32[]{:S(2)}) copy-start(bf16[1,1,256,128]{3,2,1,0:T(8,128)(2,1)} %atom_hbm.1) | copy-start | bytes 196612
  3.3 0.8 %copy-start.3 = (f32[1,1,3,32,128]{4,3,2,1,0:T(8,128)S(1)}, f32[1,1,3,32,128]{4,3,2,1,0:T(8,128)}, u32[]{:S(2)}) copy-start(f32[1,1,3,32,128]{4,3,2,1,0:T(8,128)} %disp_hbm.1) | copy-start | bytes 147460
  4.1 0.7 %copy-start.4 = (f32[3,16,128]{2,1,0:T(8,128)S(1)}, f32[3,16,128]{2,1,0:T(8,128)}, u32[]{:S(2)}) copy-start(f32[3,16,128]{2,1,0:T(8,128)} %rw_hbm.1) | copy-start | bytes 73732
  4.9 0.7 %copy-start.5 = (s32[1,1,32,128]{3,2,1,0:T(8,128)S(1)}, s32[1,1,32,128]{3,2,1,0:T(8,128)}, u32[]{:S(2)}) copy-start(s32[1,1,32,128]{3,2,1,0:T(8,128)} %nbr_hbm.1) | copy-start | bytes 49156
  5.6 0.7 %copy-start.6 = (s32[1,1,128]{2,1,0:T(1,128)S(1)}, s32[1,1,128]{2,1,0:T(1,128)}, u32[]{:S(2)}) copy-start(s32[1,1,128]{2,1,0:T(1,128)} %cnt_hbm.1) | copy-start | bytes 1540

commit v3 on v2

--- a/solution.py
+++ b/solution.py
@@ -14,6 +14,10 @@
 ORDER = (0, 1, 2, 6, 7, 8, 3, 5, 4)
 MESH = pl.DeviceIdType.MESH
 TILE = 16
+UNROLL = 4
+PREP = 2
+GATHER = 8
+EARLY = 6
 NT = (((1,), (1,)), ((), ()))
 F32 = jnp.float32
 BF16 = jnp.bfloat16
@@ -77,19 +81,6 @@
         tbl[h * ch:(h + 1) * ch, own] = (
             atom_ref[0, 0, h * hb:(h + 1) * hb, :].astype(F32).T.astype(BF16)
         )
-    pl.semaphore_wait(barrier, len(peers))
-
-    halo = []
-    for pos in range(8):
-        s = ORDER[pos]
-        dg, db = s // 3 - 1, s % 3 - 1
-        halo.append(pltpu.make_async_remote_copy(
-            src_ref=tbl.at[:, own], dst_ref=tbl.at[:, pl.ds(pos * hb, hb)],
-            send_sem=halo_s.at[pos], recv_sem=halo_r.at[pos],
-            device_id=at(-dg, -db), device_id_type=MESH))
-    for c in halo:
-        c.start()
-
     for c in loads[1:]:
         c.wait()
     n = nbr_ref[0, 0]
@@ -138,8 +129,8 @@
         return pl.ds(pl.multiple_of(k * npr, npr), count * npr)
 
     def prepare(c, carry):
-        for j in range(2):
-            k = c * 2 + j
+        for j in range(PREP):
+            k = c * PREP + j
             at_k = lanes_of(k)
             off = dist[pl.ds(k, 1), :] - centres
             shaped = jnp.exp(-sharp * (off * off)) * env[pl.ds(k, 1), :]
@@ -150,26 +141,41 @@
             for pos in range(9):
                 row = jnp.broadcast_to(key[pos, pl.ds(k, 1), :], (hb, npr)).astype(BF16)
                 oh[pos * hb:(pos + 1) * hb, at_k] = jnp.where(lines == row, one, zero)
-        rad = dot(wt[:, 0:3 * nb], basis[:, lanes_of(c * 2, 2)])
-        for j in range(2):
-            radial[c * 2 + j] = rad[:, j * npr:(j + 1) * npr]
+        rad = dot(wt[:, 0:3 * nb], basis[:, lanes_of(c * PREP, PREP)])
+        for j in range(PREP):
+            radial[c * PREP + j] = rad[:, j * npr:(j + 1) * npr]
         return carry
 
-    lax.fori_loop(0, nk // 2, prepare, 0)
-
+    lax.fori_loop(0, EARLY, prepare, 0)
+
+    pl.semaphore_wait(barrier, len(peers))
+
+    halo = []
+    for pos in range(8):
+        s = ORDER[pos]
+        dg, db = s // 3 - 1, s % 3 - 1
+        halo.append(pltpu.make_async_remote_copy(
+            src_ref=tbl.at[:, own], dst_ref=tbl.at[:, pl.ds(pos * hb, hb)],
+            send_sem=halo_s.at[pos], recv_sem=halo_r.at[pos],
+            device_id=at(-dg, -db), device_id_type=MESH))
     for c in halo:
+        c.start()
+
+    lax.fori_loop(EARLY, nk // PREP, prepare, 0)
+
+    for c in halo:
         c.wait_recv()
 
     def gather(c, carry):
-        both = dot(tbl[...], oh[:, lanes_of(c * 2, 2)])
-        for j in range(2):
-            k = c * 2 + j
+        both = dot(tbl[...], oh[:, lanes_of(c * GATHER, GATHER)])
+        for j in range(GATHER):
+            k = c * GATHER + j
             cols = slice(j * npr, (j + 1) * npr)
             upper = half[pl.ds(k, 1), :] > 0
             feat[k] = jnp.where(upper, both[ch:, cols], both[:ch, cols])
         return carry
 
-    lax.fori_loop(0, nk // 2, gather, 0)
+    lax.fori_loop(0, nk // GATHER, gather, 0)
 
     def moment_tile(t, carry):
         at_t = pl.ds(pl.multiple_of(t * TILE, TILE), TILE)
@@ -185,7 +191,7 @@
             )
 
         acc = lax.fori_loop(0, nk, body, tuple(jnp.zeros((TILE, npr), F32) for _ in range(9)),
-                            unroll=4)
+                            unroll=UNROLL)
         for m in range(9):
             mom[at_t, m * npr:(m + 1) * npr] = acc[m].astype(BF16)
         return carry
@@ -248,7 +254,7 @@
             )
             return carry
 
-        return lax.fori_loop(0, nk, body, carry, unroll=4)
+        return lax.fori_loop(0, nk, body, carry, unroll=UNROLL)
 
     lax.fori_loop(0, ch // TILE, trace_tile, 0)
 
@@ -364,7 +370,7 @@
             jax.ShapeDtypeStruct((3, nb, ch), F32),
             jax.ShapeDtypeStruct((3, ch, ch), F32),
         ),
-        in_specs=[pl.BlockSpec(memory_space=pl.ANY)] * 7,
+        in_specs=[pl.BlockSpec(memory_space=pltpu.HBM)] * 7,
         out_specs=(vm, vm, vm),
         scratch_shapes=[
             V((2 * ch, 9 * hb), BF16),

time: 52.7 us -> 50.6 us (0.960)
  Pallas kernels: 44.1 us -> 42.1 us
    pallas_call x1, Pallas kernels: 44.1 us -> 42.1 us  [shards(): pl.pallas_call(functools.partial(kernel, ngz, nxy), out_shape=(jax.ShapeD...]
where the time goes in v3:
time: 50.6 us; the launch traced here: 50.2 us
  Pallas kernels  42.1 us (83%)
  local copies, waits for them, and re-layouts  7.53 us (15%)
  between operations  0.66 us (1%)
    pallas_call x1, Pallas kernels, shards(): pl.pallas_call(functools.partial(kernel, ngz, nxy), out_shape=(jax.ShapeD...  42.1 us
    unnamed x17, local copies, waits for them, and re-layouts  7.53 us

profile of v3, /device:TPU:0, one launch (start us, length us, event | category | flops | bytes accessed | tf_op | source)
XLA Modules:
  0.0 50.2 jit_solution(14322333648068105031)
XLA Ops:
  0.6 0.0 copy-start
  0.6 1.0 %copy-done = bf16[1,1,9,128,128]{4,3,2,1,0:T(8,128)(2,1)S(1)} copy-done((bf16[1,1,9,128,128]{4,3,2,1,0:T(8,128)(2,1)S(1)}, bf16[1,1,9,128,128]{4,3,2,1,0:T(8,128)(2,1)}, u32[]{:S(2)}) %copy-start) | copy-done | bytes 294936
  1.6 0.0 copy-start.1
  1.6 0.9 %copy-done.1 = bf16[3,128,128]{2,1,0:T(8,128)(2,1)S(1)} copy-done((bf16[3,128,128]{2,1,0:T(8,128)(2,1)S(1)}, bf16[3,128,128]{2,1,0:T(8,128)(2,1)}, u32[]{:S(2)}) %copy-start.1) | copy-done | bytes 98328
  2.5 0.0 copy-start.2
  2.5 0.8 %copy-done.2 = bf16[1,1,256,128]{3,2,1,0:T(8,128)(2,1)S(1)} copy-done((bf16[1,1,256,128]{3,2,1,0:T(8,128)(2,1)S(1)}, bf16[1,1,256,128]{3,2,1,0:T(8,128)(2,1)}, u32[]{:S(2)}) %copy-start.2) | copy-done | bytes 65560
  3.3 0.0 copy-start.3
  3.3 0.8 %copy-done.3 = f32[1,1,3,32,128]{4,3,2,1,0:T(8,128)S(1)} copy-done((f32[1,1,3,32,128]{4,3,2,1,0:T(8,128)S(1)}, f32[1,1,3,32,128]{4,3,2,1,0:T(8,128)}, u32[]{:S(2)}) %copy-start.3) | copy-done | bytes 49176
  4.1 0.0 copy-start.4
  4.1 0.7 %copy-done.4 = f32[3,16,128]{2,1,0:T(8,128)S(1)} copy-done((f32[3,16,128]{2,1,0:T(8,128)S(1)}, f32[3,16,128]{2,1,0:T(8,128)}, u32[]{:S(2)}) %copy-start.4) | copy-done | bytes 24600
  4.9 0.0 copy-start.5
  4.9 0.7 %copy-done.5 = s32[1,1,32,128]{3,2,1,0:T(8,128)S(1)} copy-done((s32[1,1,32,128]{3,2,1,0:T(8,128)S(1)}, s32[1,1,32,128]{3,2,1,0:T(8,128)}, u32[]{:S(2)}) %copy-start.5) | copy-done | bytes 16408
  5.6 0.0 copy-start.6
  5.6 0.7 %copy-done.6 = s32[1,1,128]{2,1,0:T(1,128)S(1)} copy-done((s32[1,1,128]{2,1,0:T(1,128)S(1)}, s32[1,1,128]{2,1,0:T(1,128)}, u32[]{:S(2)}) %copy-start.6) | copy-done | bytes 536
  6.2 42.1 %shard_map.94 = (f32[1,1,256,128]{3,2,1,0:T(8,128)S(1)}, f32[3,16,128]{2,1,0:T(8,128)S(1)}, f32[3,128,128]{2,1,0:T(8,128)S(1)}) custom-call(bf16[1,1,9,128,128]{4,3,2,1,0:T(8,128)(2,1)S(1)} %copy-done, f32[1,1,3,32,128]{4,3,2,1,0:T(8,128)S(1)} %copy-done.3, s32[1,1,32,128]{3,2,1,0:T(8,128)S(1)} %copy-done.5, s32[1,1,128]{2,1,0:T(1,128)S(1)} %copy-done.6, ...), custom_call_target="tpu_custom_call" | custom-call | tf_op jit(solution)/shard_map/pallas_call | solution.py:366
  48.3 0.7 %copy.13 = f32[1,1,256,128]{3,2,1,0:T(8,128)} copy(f32[1,1,256,128]{3,2,1,0:T(8,128)S(1)} %get-tuple-element.6) | data formatting | bytes 262144
  49.0 0.6 %copy.14 = f32[3,16,128]{2,1,0:T(8,128)} copy(f32[3,16,128]{2,1,0:T(8,128)S(1)} %get-tuple-element.7) | data formatting | bytes 49152
  49.6 0.7 %copy.15 = f32[3,128,128]{2,1,0:T(8,128)} copy(f32[3,128,128]{2,1,0:T(8,128)S(1)} %get-tuple-element.8) | data formatting | bytes 393216
Async XLA Ops:
  0.6 1.0 %copy-start = (bf16[1,1,9,128,128]{4,3,2,1,0:T(8,128)(2,1)S(1)}, bf16[1,1,9,128,128]{4,3,2,1,0:T(8,128)(2,1)}, u32[]{:S(2)}) copy-start(bf16[1,1,9,128,128]{4,3,2,1,0:T(8,128)(2,1)} %cot_hbm.1) | copy-start | bytes 884740
  1.6 0.9 %copy-start.1 = (bf16[3,128,128]{2,1,0:T(8,128)(2,1)S(1)}, bf16[3,128,128]{2,1,0:T(8,128)(2,1)}, u32[]{:S(2)}) copy-start(bf16[3,128,128]{2,1,0:T(8,128)(2,1)} %mw_hbm.1) | copy-start | bytes 294916
  2.5 0.8 %copy-start.2 = (bf16[1,1,256,128]{3,2,1,0:T(8,128)(2,1)S(1)}, bf16[1,1,256,128]{3,2,1,0:T(8,128)(2,1)}, u32[]{:S(2)}) copy-start(bf16[1,1,256,128]{3,2,1,0:T(8,128)(2,1)} %atom_hbm.1) | copy-start | bytes 196612
  3.3 0.8 %copy-start.3 = (f32[1,1,3,32,128]{4,3,2,1,0:T(8,128)S(1)}, f32[1,1,3,32,128]{4,3,2,1,0:T(8,128)}, u32[]{:S(2)}) copy-start(f32[1,1,3,32,128]{4,3,2,1,0:T(8,128)} %disp_hbm.1) | copy-start | bytes 147460
  4.1 0.7 %copy-start.4 = (f32[3,16,128]{2,1,0:T(8,128)S(1)}, f32[3,16,128]{2,1,0:T(8,128)}, u32[]{:S(2)}) copy-start(f32[3,16,128]{2,1,0:T(8,128)} %rw_hbm.1) | copy-start | bytes 73732
  4.9 0.7 %copy-start.5 = (s32[1,1,32,128]{3,2,1,0:T(8,128)S(1)}, s32[1,1,32,128]{3,2,1,0:T(8,128)}, u32[]{:S(2)}) copy-start(s32[1,1,32,128]{3,2,1,0:T(8,128)} %nbr_hbm.1) | copy-start | bytes 49156
  5.6 0.7 %copy-start.6 = (s32[1,1,128]{2,1,0:T(1,128)S(1)}, s32[1,1,128]{2,1,0:T(1,128)}, u32[]{:S(2)}) copy-start(s32[1,1,128]{2,1,0:T(1,128)} %cnt_hbm.1) | copy-start | bytes 1540

commit v4 on v3

--- a/solution.py
+++ b/solution.py
@@ -13,11 +13,11 @@
 LEVEL_OF = (0, 1, 1, 1, 2, 2, 2, 2, 2)
 ORDER = (0, 1, 2, 6, 7, 8, 3, 5, 4)
 MESH = pl.DeviceIdType.MESH
-TILE = 16
-UNROLL = 4
-PREP = 2
-GATHER = 8
-EARLY = 6
+TILE = 32
+UNROLL = 8
+PREP = 4
+GATHER = 16
+EARLY = 3
 NT = (((1,), (1,)), ((), ()))
 F32 = jnp.float32
 BF16 = jnp.bfloat16
@@ -158,24 +158,31 @@
             src_ref=tbl.at[:, own], dst_ref=tbl.at[:, pl.ds(pos * hb, hb)],
             send_sem=halo_s.at[pos], recv_sem=halo_r.at[pos],
             device_id=at(-dg, -db), device_id_type=MESH))
-    for c in halo:
+    for c in halo[5:] + halo[:5]:
         c.start()
 
     lax.fori_loop(EARLY, nk // PREP, prepare, 0)
 
-    for c in halo:
-        c.wait_recv()
-
-    def gather(c, carry):
-        both = dot(tbl[...], oh[:, lanes_of(c * GATHER, GATHER)])
-        for j in range(GATHER):
-            k = c * GATHER + j
-            cols = slice(j * npr, (j + 1) * npr)
-            upper = half[pl.ds(k, 1), :] > 0
-            feat[k] = jnp.where(upper, both[ch:, cols], both[:ch, cols])
-        return carry
-
-    lax.fori_loop(0, nk // GATHER, gather, 0)
+    def gather(first, last, more):
+        def step(c, carry):
+            both = dot(tbl[:, first * hb:last * hb],
+                       oh[first * hb:last * hb, lanes_of(c * GATHER, GATHER)])
+            for j in range(GATHER):
+                k = c * GATHER + j
+                cols = slice(j * npr, (j + 1) * npr)
+                upper = half[pl.ds(k, 1), :] > 0
+                got = jnp.where(upper, both[ch:, cols], both[:ch, cols])
+                feat[k] = feat[k] + got if more else got
+            return carry
+
+        lax.fori_loop(0, nk // GATHER, step, 0)
+
+    for c in halo[5:]:
+        c.wait_recv()
+    gather(5, 9, False)
+    for c in halo[:5]:
+        c.wait_recv()
+    gather(0, 5, True)
 
     def moment_tile(t, carry):
         at_t = pl.ds(pl.multiple_of(t * TILE, TILE), TILE)
@@ -258,31 +265,6 @@
 
     lax.fori_loop(0, ch // TILE, trace_tile, 0)
 
-    rad = dot_nt(basis[...], ft[...])
-    rad = rad[0:nb] + rad[2 * nb:3 * nb]
-    for l in range(3):
-        radgz[g, l] = rad[:, l * ch:(l + 1) * ch].astype(BF16)
-    rgz = []
-    for d in range(1, ngz):
-        rgz.append(pltpu.make_async_remote_copy(
-            src_ref=radgz.at[g], dst_ref=radgz.at[g],
-            send_sem=rgz_s.at[d], recv_sem=rgz_r.at[d],
-            device_id=at(d, 0), device_id_type=MESH))
-    for c in rgz:
-        c.start()
-
-    for c in mrs:
-        c.wait_recv()
-    mixgz[g] = added(mixrs).astype(mixgz.dtype)
-    mgz = []
-    for d in range(1, ngz):
-        mgz.append(pltpu.make_async_remote_copy(
-            src_ref=mixgz.at[g], dst_ref=mixgz.at[g],
-            send_sem=mgz_s.at[d], recv_sem=mgz_r.at[d],
-            device_id=at(d, 0), device_id_type=MESH))
-    for c in mgz:
-        c.start()
-
     back = []
 
     def scatter(first, last):
@@ -301,6 +283,33 @@
 
     scatter(0, 3)
 
+    rad = dot_nt(basis[...], ft[...])
+    rad = rad[0:nb] + rad[2 * nb:3 * nb]
+    for l in range(3):
+        radgz[g, l] = rad[:, l * ch:(l + 1) * ch].astype(BF16)
+    rgz = []
+    for d in range(1, ngz):
+        rgz.append(pltpu.make_async_remote_copy(
+            src_ref=radgz.at[g], dst_ref=radgz.at[g],
+            send_sem=rgz_s.at[d], recv_sem=rgz_r.at[d],
+            device_id=at(d, 0), device_id_type=MESH))
+    for c in rgz:
+        c.start()
+
+    for c in mrs:
+        c.wait_recv()
+    mixgz[g] = added(mixrs).astype(mixgz.dtype)
+    mgz = []
+    for d in range(1, ngz):
+        mgz.append(pltpu.make_async_remote_copy(
+            src_ref=mixgz.at[g], dst_ref=mixgz.at[g],
+            send_sem=mgz_s.at[d], recv_sem=mgz_r.at[d],
+            device_id=at(d, 0), device_id_type=MESH))
+    for c in mgz:
+        c.start()
+
+    scatter(3, 6)
+
     for c in rgz:
         c.wait_recv()
     radxy[b] = added(radgz).astype(BF16)
@@ -312,8 +321,6 @@
             device_id=at(0, d), device_id_type=MESH))
     for c in rxy:
         c.start()
-
-    scatter(3, 6)
 
     for c in mgz:
         c.wait_recv()

time: 50.6 us -> 48.9 us (0.966)
  Pallas kernels: 42.1 us -> 40.3 us
    pallas_call x1, Pallas kernels: 42.1 us -> 40.3 us  [shards(): pl.pallas_call(functools.partial(kernel, ngz, nxy), out_shape=(jax.ShapeD...]
where the time goes in v4:
time: 48.9 us; the launch traced here: 48.4 us
  Pallas kernels  40.3 us (82%)
  local copies, waits for them, and re-layouts  7.53 us (15%)
  between operations  0.66 us (1%)
    pallas_call x1, Pallas kernels, shards(): pl.pallas_call(functools.partial(kernel, ngz, nxy), out_shape=(jax.ShapeD...  40.3 us
    unnamed x17, local copies, waits for them, and re-layouts  7.53 us

profile of v4, /device:TPU:0, one launch (start us, length us, event | category | flops | bytes accessed | tf_op | source)
XLA Modules:
  0.0 48.4 jit_solution(2554270248770645928)
XLA Ops:
  0.6 0.0 copy-start
  0.6 1.0 %copy-done = bf16[1,1,9,128,128]{4,3,2,1,0:T(8,128)(2,1)S(1)} copy-done((bf16[1,1,9,128,128]{4,3,2,1,0:T(8,128)(2,1)S(1)}, bf16[1,1,9,128,128]{4,3,2,1,0:T(8,128)(2,1)}, u32[]{:S(2)}) %copy-start) | copy-done | bytes 294936
  1.6 0.0 copy-start.1
  1.6 0.9 %copy-done.1 = bf16[3,128,128]{2,1,0:T(8,128)(2,1)S(1)} copy-done((bf16[3,128,128]{2,1,0:T(8,128)(2,1)S(1)}, bf16[3,128,128]{2,1,0:T(8,128)(2,1)}, u32[]{:S(2)}) %copy-start.1) | copy-done | bytes 98328
  2.5 0.0 copy-start.2
  2.5 0.8 %copy-done.2 = bf16[1,1,256,128]{3,2,1,0:T(8,128)(2,1)S(1)} copy-done((bf16[1,1,256,128]{3,2,1,0:T(8,128)(2,1)S(1)}, bf16[1,1,256,128]{3,2,1,0:T(8,128)(2,1)}, u32[]{:S(2)}) %copy-start.2) | copy-done | bytes 65560
  3.3 0.0 copy-start.3
  3.3 0.8 %copy-done.3 = f32[1,1,3,32,128]{4,3,2,1,0:T(8,128)S(1)} copy-done((f32[1,1,3,32,128]{4,3,2,1,0:T(8,128)S(1)}, f32[1,1,3,32,128]{4,3,2,1,0:T(8,128)}, u32[]{:S(2)}) %copy-start.3) | copy-done | bytes 49176
  4.1 0.0 copy-start.4
  4.1 0.7 %copy-done.4 = f32[3,16,128]{2,1,0:T(8,128)S(1)} copy-done((f32[3,16,128]{2,1,0:T(8,128)S(1)}, f32[3,16,128]{2,1,0:T(8,128)}, u32[]{:S(2)}) %copy-start.4) | copy-done | bytes 24600
  4.9 0.0 copy-start.5
  4.9 0.7 %copy-done.5 = s32[1,1,32,128]{3,2,1,0:T(8,128)S(1)} copy-done((s32[1,1,32,128]{3,2,1,0:T(8,128)S(1)}, s32[1,1,32,128]{3,2,1,0:T(8,128)}, u32[]{:S(2)}) %copy-start.5) | copy-done | bytes 16408
  5.6 0.0 copy-start.6
  5.6 0.7 %copy-done.6 = s32[1,1,128]{2,1,0:T(1,128)S(1)} copy-done((s32[1,1,128]{2,1,0:T(1,128)S(1)}, s32[1,1,128]{2,1,0:T(1,128)}, u32[]{:S(2)}) %copy-start.6) | copy-done | bytes 536
  6.2 40.3 %shard_map.94 = (f32[1,1,256,128]{3,2,1,0:T(8,128)S(1)}, f32[3,16,128]{2,1,0:T(8,128)S(1)}, f32[3,128,128]{2,1,0:T(8,128)S(1)}) custom-call(bf16[1,1,9,128,128]{4,3,2,1,0:T(8,128)(2,1)S(1)} %copy-done, f32[1,1,3,32,128]{4,3,2,1,0:T(8,128)S(1)} %copy-done.3, s32[1,1,32,128]{3,2,1,0:T(8,128)S(1)} %copy-done.5, s32[1,1,128]{2,1,0:T(1,128)S(1)} %copy-done.6, ...), custom_call_target="tpu_custom_call" | custom-call | tf_op jit(solution)/shard_map/pallas_call | solution.py:373
  46.5 0.7 %copy.13 = f32[1,1,256,128]{3,2,1,0:T(8,128)} copy(f32[1,1,256,128]{3,2,1,0:T(8,128)S(1)} %get-tuple-element.6) | data formatting | bytes 262144
  47.2 0.6 %copy.14 = f32[3,16,128]{2,1,0:T(8,128)} copy(f32[3,16,128]{2,1,0:T(8,128)S(1)} %get-tuple-element.7) | data formatting | bytes 49152
  47.8 0.7 %copy.15 = f32[3,128,128]{2,1,0:T(8,128)} copy(f32[3,128,128]{2,1,0:T(8,128)S(1)} %get-tuple-element.8) | data formatting | bytes 393216
Async XLA Ops:
  0.6 1.0 %copy-start = (bf16[1,1,9,128,128]{4,3,2,1,0:T(8,128)(2,1)S(1)}, bf16[1,1,9,128,128]{4,3,2,1,0:T(8,128)(2,1)}, u32[]{:S(2)}) copy-start(bf16[1,1,9,128,128]{4,3,2,1,0:T(8,128)(2,1)} %cot_hbm.1) | copy-start | bytes 884740
  1.6 0.9 %copy-start.1 = (bf16[3,128,128]{2,1,0:T(8,128)(2,1)S(1)}, bf16[3,128,128]{2,1,0:T(8,128)(2,1)}, u32[]{:S(2)}) copy-start(bf16[3,128,128]{2,1,0:T(8,128)(2,1)} %mw_hbm.1) | copy-start | bytes 294916
  2.5 0.8 %copy-start.2 = (bf16[1,1,256,128]{3,2,1,0:T(8,128)(2,1)S(1)}, bf16[1,1,256,128]{3,2,1,0:T(8,128)(2,1)}, u32[]{:S(2)}) copy-start(bf16[1,1,256,128]{3,2,1,0:T(8,128)(2,1)} %atom_hbm.1) | copy-start | bytes 196612
  3.3 0.8 %copy-start.3 = (f32[1,1,3,32,128]{4,3,2,1,0:T(8,128)S(1)}, f32[1,1,3,32,128]{4,3,2,1,0:T(8,128)}, u32[]{:S(2)}) copy-start(f32[1,1,3,32,128]{4,3,2,1,0:T(8,128)} %disp_hbm.1) | copy-start | bytes 147460
  4.1 0.7 %copy-start.4 = (f32[3,16,128]{2,1,0:T(8,128)S(1)}, f32[3,16,128]{2,1,0:T(8,128)}, u32[]{:S(2)}) copy-start(f32[3,16,128]{2,1,0:T(8,128)} %rw_hbm.1) | copy-start | bytes 73732
  4.9 0.7 %copy-start.5 = (s32[1,1,32,128]{3,2,1,0:T(8,128)S(1)}, s32[1,1,32,128]{3,2,1,0:T(8,128)}, u32[]{:S(2)}) copy-start(s32[1,1,32,128]{3,2,1,0:T(8,128)} %nbr_hbm.1) | copy-start | bytes 49156
  5.6 0.7 %copy-start.6 = (s32[1,1,128]{2,1,0:T(1,128)S(1)}, s32[1,1,128]{2,1,0:T(1,128)}, u32[]{:S(2)}) copy-start(s32[1,1,128]{2,1,0:T(1,128)} %cnt_hbm.1) | copy-start | bytes 1540
